TPU v7x, 1024 devices: a whole 8x8x8 slice. The times are simulated.
1024 devices in a mesh: grp: 128 (over y, z_lo, x), tp: 8 (over z_hi, core).
Axes of the slice: x: 8, y: 8, z: 8 (z_hi: 4, z_lo: 2; z = z_hi * 2 + z_lo), core: 2. Of those that a mesh axis runs over, the one named last changes fastest.
Arguments:
- tokens: bfloat16 [1024, 4096], P('grp', 'tp'), may hold values from -6 to 6
- expert_ids: int32 [1024, 8], replicated, may hold values from 0 to 127, all different within a row; in each aligned block of 1024 rows (0 to 1023, 1024 to 2047, ...) at most 160 rows name the same one
- route_weight: float32 [1024, 8], replicated, may hold values from 0.1 to 1
- owner: int32 [128], replicated, may hold values from 0 to 127, each once
- gate_weight: bfloat16 [128, 4096, 1024], P('grp', 'tp'), may hold values from -0.09375 to 0.09375
- up_weight: bfloat16 [128, 4096, 1024], P('grp', 'tp'), may hold values from -0.09375 to 0.09375
- down_weight: bfloat16 [128, 1024, 4096], P('grp', None, 'tp'), may hold values from -0.1875 to 0.1875
Outputs:
- mixed: bfloat16 [1024, 4096], P('grp', 'tp')
Inputs may be any that keep to these rules, and one draw needn't show every extreme that they name: `expert_ids`: each row names 8 different experts; no expert is named by more than 160 rows, a bound that some block reaches. `owner`: A permutation: every group owns exactly one expert.
All inputs are finite; a program needn't handle non-finite values.
Results may differ from a plain program's by a relative error of at most 0.0055.
Values may be sent and summed in bfloat16 or wider, within the bound.
A program may use at most 32 MiB of HBM per device.

v0:
```python
import jax
import jax.numpy as jnp
from jax import lax
from jax.sharding import PartitionSpec as P


def on_device(tokens, expert_ids, route_weight, owner, gate_weight, up_weight, down_weight):
    group = lax.axis_index("grp")
    local_rows = tokens.shape[0]
    total_rows = expert_ids.shape[0]
    capacity = min(20 * local_rows, total_rows)
    row_index = jnp.arange(total_rows, dtype=jnp.int32)
    mine = jnp.sum(jnp.where(owner == group, jnp.arange(owner.shape[0], dtype=jnp.int32), 0))
    hit = expert_ids == mine
    taken = jnp.any(hit, axis=1)
    weight = jnp.sum(jnp.where(hit, route_weight, jnp.float32(0.0)), axis=1)
    place = jnp.cumsum(taken.astype(jnp.int32)) - 1
    slot_index = jnp.arange(capacity, dtype=jnp.int32)
    match = (place[None, :] == slot_index[:, None]) & taken[None, :]
    slot_row = jnp.sum(jnp.where(match, row_index[None, :], 0), axis=1)
    valid = jnp.any(match, axis=1)
    slot_weight = jnp.where(valid, weight[slot_row], jnp.float32(0.0))
    empty = jnp.zeros((capacity, tokens.shape[1]), jnp.bfloat16)
    piece = lax.all_gather(tokens, "grp", axis=0, tiled=True)
    offset = slot_row
    inside = valid & (offset >= 0) & (offset < piece.shape[0])
    chosen = jnp.take(piece, jnp.clip(offset, 0, piece.shape[0] - 1), axis=0)
    selected = jnp.where(inside[:, None], chosen, empty)
    gate_part = jnp.dot(selected, gate_weight[0], preferred_element_type=jnp.float32)
    up_part = jnp.dot(selected, up_weight[0], preferred_element_type=jnp.float32)
    gate, up = lax.psum((gate_part, up_part), "tp")
    hidden = (jax.nn.silu(gate) * up).astype(jnp.bfloat16)
    output = jnp.dot(hidden, down_weight[0], preferred_element_type=jnp.float32)
    weighted = output * slot_weight[:, None]
    offset = slot_row
    inside = valid & (offset >= 0) & (offset < local_rows * lax.axis_size("grp"))
    target = jnp.where(inside, offset, local_rows * lax.axis_size("grp"))
    buffer = jnp.zeros((local_rows * lax.axis_size("grp"), weighted.shape[1]), jnp.float32)
    mixed = lax.psum_scatter(
        buffer.at[target].add(weighted, mode="drop"), "grp", scatter_dimension=0, tiled=True
    )
    return mixed.astype(jnp.bfloat16)


def solution(mesh):
    return jax.shard_map(
        on_device,
        mesh=mesh,
        in_specs=(
            P("grp", "tp"),
            P(),
            P(),
            P(),
            P("grp", "tp", None),
            P("grp", "tp", None),
            P("grp", None, "tp"),
        ),
        out_specs=P("grp", "tp"),
        check_vma=False,
    )
```

profile of v0, /device:TPU:256, one launch (start us, length us, event | category | flops | bytes accessed | tf_op | source)
XLA Modules:
  0.0 1328.5 jit_solution(7815883793523639264)
XLA Ops:
  6.5 0.0 copy-start
  6.5 0.0 copy-start.1
  6.5 0.0 all-gather.2.cloned.1.call-start
  6.5 0.7 all-gather.2.cloned.1.call-update
  7.3 0.0 all-reduce.3.cloned.1.call-start
  7.3 1.3 fusion.10
  8.6 1.4 select_reduce_fusion.1
  10.1 0.3 reduce-window.9
  10.4 0.1 slice.7
  10.5 0.1 slice_reduce_fusion
  10.6 0.1 add_bitcast_fusion
  10.7 0.2 fusion.8
  10.8 0.2 select_reduce_fusion
  11.1 589.8 %all-gather.2.cloned.1.call-done = bf16[1024,512]{1,0:T(8,128)(2,1)} async-done(((bf16[8,512]{1,0:T(8,128)(2,1)}), bf16[1024,512]{1,0:T(8,128)(2,1)}) %all-gather.2.cloned.1.call-update) | async-done | bytes 1048592 | tf_op jit(solution)/shard_map/all_gather | solution.py:24
  600.9 2.3 gather_fusion
  603.2 0.0 copy-done
  603.2 1.2 fusion.1
  604.5 0.0 copy-done.1
  604.5 0.0 copy-start.2
  604.5 1.2 fusion.3
  605.7 0.0 all-reduce.3.cloned.1.call-update
  605.7 0.0 reduce-scatter.2.cloned.1.call-start
  605.8 1.2 gather_fusion.1
  607.0 81.5 %all-reduce.3.cloned.1.call-done = (f32[160,1024]{1,0:T(8,128)}, f32[160,1024]{1,0:T(8,128)}) async-done(((f32[160,1024]{1,0:T(8,128)}, f32[160,1024]{1,0:T(8,128)}), (f32[160,1024]{1,0:T(8,128)}, f32[160,1024]{1,0:T(8,128)})) %all-reduce.3.cloned.1.call-update) | async-done | bytes 1310736 | tf_op jit(solution)/shard_map/psum | solution.py:31
  688.5 0.0 copy-done.2
  688.5 1.7 convolution_multiply_fusion
  690.2 3.0 scatter_custom_fusion
  693.1 0.0 reduce-scatter.2.cloned.1.call-update
  693.2 627.5 %reduce-scatter.2.cloned.1.call-done = f32[8,512]{1,0:T(8,128)} async-done(((f32[1024,512]{1,0:T(8,128)}), f32[8,512]{1,0:T(8,128)}) %reduce-scatter.2.cloned.1.call-update) | async-done | bytes 16400 | tf_op jit(solution)/shard_map/reduce_scatter | solution.py:39
  1320.6 1.3 convert_element_type.16
  (8 shorter events, 0.1 us)
Async XLA Ops:
  6.5 596.7 %copy-start = (bf16[1,512,1024]{2,1,0:T(8,128)(2,1)S(1)}, bf16[1,512,1024]{2,1,0:T(8,128)(2,1)}, u32[]{:S(2)}) copy-start(bf16[1,512,1024]{2,1,0:T(8,128)(2,1)} %param.12) | copy-start | bytes 3145732
  6.5 598.0 %copy-start.1 = (bf16[1,512,1024]{2,1,0:T(8,128)(2,1)S(1)}, bf16[1,512,1024]{2,1,0:T(8,128)(2,1)}, u32[]{:S(2)}) copy-start(bf16[1,512,1024]{2,1,0:T(8,128)(2,1)} %param.11) | copy-start | bytes 3145732
  6.5 594.4 %all-gather.2.cloned.1.call-start = ((), (), s32[]{:S(2)}) async-start(), calls=%async_computation.1 | async-start | bytes 1056768 | tf_op jit(solution)/shard_map/all_gather | solution.py:24
  7.3 681.2 %all-reduce.3.cloned.1.call-start = ((), (), s32[]{:S(2)}) async-start(), calls=%async_computation.3 | async-start | bytes 2621440 | tf_op jit(solution)/shard_map/psum | solution.py:31
  604.5 84.0 %copy-start.2 = (bf16[1,1024,512]{2,1,0:T(8,128)(2,1)S(1)}, bf16[1,1024,512]{2,1,0:T(8,128)(2,1)}, u32[]{:S(2)}) copy-start(bf16[1,1024,512]{2,1,0:T(8,128)(2,1)} %param.13) | copy-start | bytes 3145732
  605.7 714.9 %reduce-scatter.2.cloned.1.call-start = ((), (), s32[]{:S(2)}) async-start(), calls=%async_computation.2 | async-start | bytes 2113536 | tf_op jit(solution)/shard_map/reduce_scatter | solution.py:39
Sparse Core Ops, SparseCore 0:
  10.0 590.8 all-gather.1
  605.9 82.5 all-reduce.2
  693.3 627.2 reduce-scatter.1
where the time goes:
time: 1330 us
  waiting for transfers between devices  1300 us (98%)
    reduce_scatter x1, waiting for transfers between devices, on_device(): lax.psum_scatter(buffer.at[target].add(weighted, mode='drop'), 'grp', sca...  627 us
    all_gather x1, waiting for transfers between devices, on_device(): piece = lax.all_gather(tokens, 'grp', axis=0, tiled=True)  590 us
    psum x1, waiting for transfers between devices, on_device(): gate, up = lax.psum((gate_part, up_part), 'tp')  81.5 us
  transfers between devices with their start and end apart: 3, of which 3 were waited for; matrix products, arithmetic and copies ran while one was open for 0% of the time, Pallas kernels for 0%

commit v1 on v0

v1 whole, which is shorter than its diff:
```python
import functools
import math

import jax
import jax.numpy as jnp
from jax import lax
from jax.experimental import pallas as pl
from jax.experimental.pallas import tpu as pltpu
from jax.sharding import PartitionSpec as P

BF16, F32, I32 = jnp.bfloat16, jnp.float32, jnp.int32
MESH = pl.DeviceIdType.MESH


def kernel(n, zhi, cap, ids_ref, rw_ref, owner_ref, tok_ref, gate_ref, up_ref, down_ref, out_ref,
           w1, w2, zbuf, tok, sel, wcol, hid, psend, precv, zsend, zrecv, acc, rbuf, tot, fsend, frecv,
           yrecv,
           w_sem, d_sem, z_send, z_recv, f_send, f_recv, s_send, s_recv, c_send, c_recv, q_send, q_recv,
           h_send, h_recv, k_send, k_recv, r_send, r_recv, g_send, g_recv, y_send, y_recv):
    rows, feat = tok_ref.shape
    ff = down_ref.shape[1]
    half = ff // 2
    part = half // zhi
    pair = 2 * rows
    block = n * pair
    chunk = block // 2
    total_rows = n * block
    grp, tp = lax.axis_index("grp"), lax.axis_index("tp")
    x, zlo, y = lax.rem(grp, n), lax.rem(lax.div(grp, n), 2), lax.div(grp, 2 * n)
    zh, core = lax.div(tp, 2), lax.rem(tp, 2)
    f = x * (1 - core) + y * core
    s = y * (1 - core) + x * core

    def at(f_, s_, z_):
        y_ = s_ * (1 - core) + f_ * core
        x_ = f_ * (1 - core) + s_ * core
        return ((y_ * 2 + z_) * n + x_, tp)

    f_peer = [None] + [at(lax.rem(f + k, n), s, zlo) for k in range(1, n)]
    s_peer = {1: at(f, lax.rem(s + 1, n), zlo), -1: at(f, lax.rem(s + n - 1, n), zlo)}
    z_peer = at(f, s, 1 - zlo)
    sibling = (grp, zh * 2 + (1 - core))
    q_peer = [None] + [(grp, lax.rem(zh + j, zhi) * 2 + core) for j in range(1, zhi)]

    def send(src, dst, ssem, rsem, device):
        copy = pltpu.make_async_remote_copy(src_ref=src, dst_ref=dst, send_sem=ssem, recv_sem=rsem,
                                            device_id=device, device_id_type=MESH)
        copy.start()
        return copy

    def arrived(dst, ssem, rsem, device):
        pltpu.make_async_remote_copy(src_ref=dst, dst_ref=dst, send_sem=ssem, recv_sem=rsem,
                                     device_id=device, device_id_type=MESH).wait_recv()

    sent = []

    loads = []
    for slot in range(2):
        side = (1 - core) if slot == 0 else core
        for q in range(zhi):
            for m, ref in enumerate((gate_ref, up_ref)):
                column = pl.multiple_of(side * half + q * part, part)
                load = pltpu.make_async_copy(ref.at[0, :, pl.ds(column, part)],
                                             w1.at[slot, q, :, pl.ds(m * part, part)], w_sem.at[slot, q, m])
                load.start()
                loads.append(load)
    load_down = pltpu.make_async_copy(down_ref.at[0], w2, d_sem)
    load_down.start()

    peers = f_peer[1:] + [s_peer[1], s_peer[-1], z_peer, sibling] + q_peer[1:]
    barrier = pltpu.get_barrier_semaphore()
    for peer in peers:
        pl.semaphore_signal(barrier, inc=1, device_id=peer, device_id_type=MESH)
    pl.semaphore_wait(barrier, len(peers))

    mine8 = pl.ds(pl.multiple_of(zlo * rows, rows), rows)
    zbuf[mine8, :] = tok_ref[...].astype(F32)
    sent.append(send(zbuf.at[mine8], zbuf.at[mine8], z_send, z_recv, z_peer))
    arrived(zbuf.at[pl.ds(pl.multiple_of((1 - zlo) * rows, rows), rows)], z_send, z_recv, z_peer)

    def at16(s_, f_):
        return pl.ds(pl.multiple_of(s_ * block + f_ * pair, pair), pair)

    tok[at16(s, f), :] = zbuf[...].astype(BF16)
    for k in range(1, n):
        sent.append(send(tok.at[at16(s, f)], tok.at[at16(s, f)], f_send.at[k], f_recv.at[k], f_peer[k]))

    experts = owner_ref.shape[1]
    mine = jnp.sum(jnp.where(owner_ref[...] == grp, lax.broadcasted_iota(I32, (1, experts), 1), 0),
                   axis=1, keepdims=True)
    hit = ids_ref[...] == mine
    taken = jnp.max(jnp.where(hit, 1.0, 0.0), axis=0, keepdims=True)
    weight = jnp.sum(jnp.where(hit, rw_ref[...], 0.0), axis=0, keepdims=True)
    high = weight.astype(BF16).astype(F32)
    middle = (weight - high).astype(BF16).astype(F32)
    low = weight - high - middle
    line = lax.broadcasted_iota(I32, (8, total_rows), 0)
    packed = jnp.where(line == 0, taken, jnp.where(line == 1, high, jnp.where(line == 2, middle,
                       jnp.where(line == 3, low, 0.0)))).astype(BF16)
    place_at = lax.broadcasted_iota(I32, (1, total_rows), 1)
    bits = [int(math.log2(v)) for v in (rows, 2, n, n)]
    i_ = place_at & (rows - 1)
    z_ = lax.shift_right_logical(place_at, bits[0]) & 1
    f_ = lax.shift_right_logical(place_at, bits[0] + 1) & (n - 1)
    s_ = lax.shift_right_logical(place_at, bits[0] + 1 + bits[2])
    y_ = s_ * (1 - core) + f_ * core
    x_ = f_ * (1 - core) + s_ * core
    row_of = ((y_ * 2 + z_) * n + x_) * rows + i_
    moved = jnp.zeros((8, total_rows), F32)
    place = jnp.zeros((8, total_rows), F32)
    step = min(256, total_rows)
    for base in range(0, total_rows, step):
        row = lax.broadcasted_iota(I32, (step, total_rows), 0) + base
        left = packed[:, base:base + step]
        moved += jnp.dot(left, jnp.where(row == row_of, 1.0, 0.0).astype(BF16), preferred_element_type=F32)
        place += jnp.dot(left, jnp.where(row < row_of, 1.0, 0.0).astype(BF16), preferred_element_type=F32)
    taken_at, place_of = moved[0:1], place[0:1]
    weight_at = moved[1:2] + moved[2:3] + moved[3:4]
    slot_at = lax.broadcasted_iota(I32, (cap, block), 0).astype(F32)
    weights = jnp.zeros((cap, 1), F32)
    for t in range(n):
        here = slice(t * block, (t + 1) * block)
        one = jnp.where((place_of[:, here] == slot_at) & (taken_at[:, here] > 0.5), 1.0, 0.0)
        sel[t] = one.astype(BF16)
        weights += jnp.sum(one * weight_at[:, here], axis=1, keepdims=True)
    wcol[...] = jnp.broadcast_to(weights, wcol.shape)

    for k in range(1, n):
        arrived(tok.at[at16(s, lax.rem(f + n - k, n))], f_send.at[k], f_recv.at[k], f_peer[k])

    def at_chunk(s_, c):
        return pl.ds(pl.multiple_of(s_ * block + c * chunk, chunk), chunk)

    def hops(direction, c):
        return n // 2 if (direction > 0) == (c == 0) else n // 2 - 1

    ways = [(w, direction, c) for c in range(2) for w, direction in enumerate((1, -1))]
    for w, direction, c in ways:
        if hops(direction, c) > 0:
            sent.append(send(tok.at[at_chunk(s, c)], tok.at[at_chunk(s, c)],
                             s_send.at[w, c, 0], s_recv.at[w, c, 0], s_peer[direction]))

    def rows_of(t):
        return jnp.dot(sel[t], tok[pl.ds(pl.multiple_of(t * block, block), block), :],
                       preferred_element_type=F32)

    picked = rows_of(s)
    for h in range(1, n // 2 + 1):
        for w, direction, c in ways:
            if h > hops(direction, c):
                continue
            came = at_chunk(lax.rem(s + n - direction * h, n), c)
            arrived(tok.at[came], s_send.at[w, c, h - 1], s_recv.at[w, c, h - 1], s_peer[direction])
            if h + 1 <= hops(direction, c):
                sent.append(send(tok.at[came], tok.at[came],
                                 s_send.at[w, c, h], s_recv.at[w, c, h], s_peer[direction]))
        picked += rows_of(lax.rem(s + h, n))
        if h < n // 2:
            picked += rows_of(lax.rem(s + n - h, n))
    rows_x = picked.astype(BF16)

    for load in loads:
        load.wait()
    order = [1] if zhi == 2 else [2, 1, 3]
    order = order + [0]
    for j in order:
        q = lax.rem(zh + j, zhi)
        psend[j] = jnp.dot(rows_x, w1[0, q], preferred_element_type=F32)
        sent.append(send(psend.at[j], precv.at[j], c_send.at[j], c_recv.at[j], sibling))
    own = None
    for j in order:
        q = lax.rem(zh + j, zhi)
        product = jnp.dot(rows_x, w1[1, q], preferred_element_type=F32)
        arrived(precv.at[j], c_send.at[j], c_recv.at[j], sibling)
        both = product + precv[j]
        if j == 0:
            own = both
        else:
            zsend[j] = both.astype(BF16)
            sent.append(send(zsend.at[j], zrecv.at[j], q_send.at[j], q_recv.at[j], q_peer[j]))

    for j in range(1, zhi):
        arrived(zrecv.at[j], q_send.at[j], q_recv.at[j], q_peer[j])
        own += zrecv[j].astype(F32)
    gate, up = own[:, :part], own[:, part:]
    me = core * zhi + zh
    hid[me] = (gate / (1.0 + jnp.exp(-gate)) * up).astype(BF16)

    for j in order[:-1]:
        sent.append(send(hid.at[me], hid.at[me], h_send.at[j], h_recv.at[j], q_peer[j]))
    sent.append(send(hid.at[me], hid.at[me], k_send.at[0], k_recv.at[0], sibling))
    load_down.wait()
    for j in order[:-1][::-1]:
        came = core * zhi + lax.rem(zh + zhi - j, zhi)
        arrived(hid.at[came], h_send.at[j], h_recv.at[j], q_peer[j])
        sent.append(send(hid.at[came], hid.at[came], k_send.at[j], k_recv.at[j], sibling))
    for j in range(zhi):
        came = (1 - core) * zhi + lax.rem(zh + zhi - j, zhi)
        arrived(hid.at[came], k_send.at[j], k_recv.at[j], sibling)

    hidden = jnp.concatenate([hid[m] for m in range(2 * zhi)], axis=1)
    result = jnp.dot(hidden, w2[...], preferred_element_type=F32)
    result = (result * wcol[:, 0:1]).astype(BF16)

    def spread(t):
        acc[pl.ds(pl.multiple_of(t * block, block), block), :] = lax.dot_general(
            sel[t], result, (((0,), (0,)), ((), ())), preferred_element_type=F32).astype(BF16)

    def pass_on(w, direction, c, k):
        length = hops(direction, c)
        to = lax.rem(s + 2 * n + direction * (length - k), n)
        if k > 0:
            arrived(rbuf.at[w, c, k - 1], r_send.at[w, c, k - 1], r_recv.at[w, c, k - 1], s_peer[direction])
            acc[at_chunk(to, c), :] = (acc[at_chunk(to, c), :].astype(F32) + rbuf[w, c, k - 1].astype(F32)).astype(BF16)
        sent.append(send(acc.at[at_chunk(to, c)], rbuf.at[w, c, k], r_send.at[w, c, k], r_recv.at[w, c, k],
                         s_peer[direction]))

    spread(lax.rem(s + n // 2, n))
    for w, direction, c in ways:
        if hops(direction, c) == n // 2:
            pass_on(w, direction, c, 0)
    for h in range(n // 2 - 1, 0, -1):
        spread(lax.rem(s + h, n))
        spread(lax.rem(s + n - h, n))
        if h == n // 2 - 1:
            for w, direction, c in ways:
                if hops(direction, c) == h:
                    pass_on(w, direction, c, 0)
    spread(s)
    for k in range(1, n // 2):
        for w, direction, c in ways:
            if k < hops(direction, c):
                pass_on(w, direction, c, k)
    for c in range(2):
        summed = acc[at_chunk(s, c), :].astype(F32)
        for w, direction in enumerate((1, -1)):
            k = hops(direction, c) - 1
            if k >= 0:
                arrived(rbuf.at[w, c, k], r_send.at[w, c, k], r_recv.at[w, c, k], s_peer[direction])
                summed += rbuf[w, c, k].astype(F32)
        tot[c * chunk:(c + 1) * chunk, :] = summed
        fsend[c * chunk:(c + 1) * chunk, :] = summed.astype(BF16)

    def at_pair(f_):
        return pl.ds(pl.multiple_of(f_ * pair, pair), pair)

    for k in range(1, n):
        to = at_pair(lax.rem(f + k, n))
        sent.append(send(fsend.at[to], frecv.at[k], g_send.at[k], g_recv.at[k], f_peer[k]))
    summed = tot[at_pair(f), :]
    for k in range(1, n):
        arrived(frecv.at[k], g_send.at[k], g_recv.at[k], f_peer[k])
        summed += frecv[k].astype(F32)
    zbuf2 = yrecv
    zbuf2[0:pair, :] = summed
    theirs = pl.ds(pl.multiple_of((1 - zlo) * rows, rows), rows)
    sent.append(send(zbuf2.at[theirs], zbuf2.at[pl.ds(pair, rows)], y_send, y_recv, z_peer))
    arrived(zbuf2.at[pl.ds(pair, rows)], y_send, y_recv, z_peer)
    out_ref[...] = (zbuf2[mine8, :] + zbuf2[pair:pair + rows, :]).astype(out_ref.dtype)

    for copy in sent:
        copy.wait_send()


def on_device(n, zhi, tokens, expert_ids, route_weight, owner, gate_weight, up_weight, down_weight):
    rows, feat = tokens.shape
    total_rows = expert_ids.shape[0]
    ff = gate_weight.shape[2]
    part = ff // 2 // zhi
    cap = min(20 * rows, total_rows)
    pair = 2 * rows
    block = n * pair
    chunk = block // 2
    half_ring = max(n // 2, 1)
    dma = pltpu.SemaphoreType.DMA
    vmem = pl.BlockSpec(memory_space=pltpu.VMEM)
    hbm = pl.BlockSpec(memory_space=pl.ANY)
    return pl.pallas_call(
        functools.partial(kernel, n, zhi, cap),
        out_shape=jax.ShapeDtypeStruct((rows, feat), BF16),
        in_specs=[vmem] * 4 + [hbm] * 3,
        out_specs=vmem,
        scratch_shapes=[
            pltpu.VMEM((2, zhi, feat, 2 * part), BF16),
            pltpu.VMEM((ff, feat), BF16),
            pltpu.VMEM((pair, feat), F32),
            pltpu.VMEM((total_rows, feat), BF16),
            pltpu.VMEM((n, cap, block), BF16),
            pltpu.VMEM((cap, 128), F32),
            pltpu.VMEM((2 * zhi, cap, part), BF16),
            pltpu.VMEM((zhi, cap, 2 * part), F32),
            pltpu.VMEM((zhi, cap, 2 * part), F32),
            pltpu.VMEM((zhi, cap, 2 * part), BF16),
            pltpu.VMEM((zhi, cap, 2 * part), BF16),
            pltpu.VMEM((total_rows, feat), BF16),
            pltpu.VMEM((2, 2, half_ring, chunk, feat), BF16),
            pltpu.VMEM((block, feat), F32),
            pltpu.VMEM((block, feat), BF16),
            pltpu.VMEM((n, pair, feat), BF16),
            pltpu.VMEM((pair + rows, feat), F32),
            dma((2, zhi, 2)), dma,
            dma, dma,
            dma((n,)), dma((n,)),
            dma((2, 2, half_ring)), dma((2, 2, half_ring)),
            dma((zhi,)), dma((zhi,)),
            dma((zhi,)), dma((zhi,)),
            dma((zhi,)), dma((zhi,)),
            dma((zhi,)), dma((zhi,)),
            dma((2, 2, half_ring)), dma((2, 2, half_ring)),
            dma((n,)), dma((n,)),
            dma, dma,
        ],
        compiler_params=pltpu.CompilerParams(
            collective_id=0, has_side_effects=True, vmem_limit_bytes=40 * 1024 * 1024
        ),
        cost_estimate=pl.CostEstimate(flops=2 * cap * feat * ff * 3, bytes_accessed=6 * feat * ff,
                                      transcendentals=cap * ff // 8),
    )(expert_ids.T, route_weight.T, owner.reshape(1, -1), tokens, gate_weight, up_weight, down_weight)


def solution(mesh):
    n = math.isqrt(mesh.shape["grp"] // 2)
    return jax.shard_map(
        functools.partial(on_device, n, mesh.shape["tp"] // 2),
        mesh=mesh,
        in_specs=(
            P("grp", "tp"),
            P(),
            P(),
            P(),
            P("grp", "tp", None),
            P("grp", "tp", None),
            P("grp", None, "tp"),
        ),
        out_specs=P("grp", "tp"),
        check_vma=False,
    )
```

time: 1330 us -> 94.7 us (0.07)
  the two profiles are of different devices: /device:TPU:256 before, /device:TPU:128 now
where the time goes in v1:
time: 94.7 us; the launch traced here: 94.2 us
  Pallas kernels  87.1 us (92%)
  local copies, waits for them, and re-layouts  7.14 us (8%)
    pallas_call x1, Pallas kernels, on_device(): pl.pallas_call(functools.partial(kernel, n, zhi, cap), out_shape=jax.Shap...  87.1 us
    unnamed x15, local copies, waits for them, and re-layouts  7.14 us

profile of v1, /device:TPU:128, one launch (start us, length us, event | category | flops | bytes accessed | tf_op | source)
XLA Modules:
  0.0 94.2 jit_solution(16085685771390494029)
XLA Ops:
  0.0 0.0 copy-start.6
  0.0 0.7 copy-done.6
  0.7 0.0 copy-start
  0.7 1.2 %copy-done = bf16[1,512,1024]{2,1,0:T(8,128)(2,1)S(1)} copy-done((bf16[1,512,1024]{2,1,0:T(8,128)(2,1)S(1)}, bf16[1,512,1024]{2,1,0:T(8,128)(2,1)}, u32[]{:S(2)}) %copy-start) | copy-done | bytes 1048600
  1.9 0.0 copy-start.1
  1.9 1.2 %copy-done.1 = bf16[1,512,1024]{2,1,0:T(8,128)(2,1)S(1)} copy-done((bf16[1,512,1024]{2,1,0:T(8,128)(2,1)S(1)}, bf16[1,512,1024]{2,1,0:T(8,128)(2,1)}, u32[]{:S(2)}) %copy-start.1) | copy-done | bytes 1048600
  3.1 0.0 copy-start.2
  3.1 1.2 %copy-done.2 = bf16[1,1024,512]{2,1,0:T(8,128)(2,1)S(1)} copy-done((bf16[1,1024,512]{2,1,0:T(8,128)(2,1)S(1)}, bf16[1,1024,512]{2,1,0:T(8,128)(2,1)}, u32[]{:S(2)}) %copy-start.2) | copy-done | bytes 1048600
  4.3 0.0 copy-start.3
  4.3 0.8 copy-done.3
  5.1 0.0 copy-start.4
  5.1 0.8 copy-done.4
  5.8 0.0 copy-start.5
  5.9 0.7 copy-done.5
  6.5 87.1 %shard_map.73 = bf16[8,512]{1,0:T(8,128)(2,1)S(1)} custom-call(s32[8,1024]{1,0:T(8,128)S(1)} %bitcast.3, f32[8,1024]{1,0:T(8,128)S(1)} %bitcast.4, s32[1,128]{1,0:T(1,128)S(1)} %bitcast.5, bf16[8,512]{1,0:T(8,128)(2,1)S(1)} %copy-done.5, bf16[1,512,1024]{2,1,0:T(8,128)(2,1)S(1)} %copy-done, bf16[1,512,1024]{2,1,0:T(8,128)(2,1)S(1)} %copy-done.1, ...), custom_call_target="tpu_custom_call" | custom-call | flops 503316480 | bytes 3145728 | tf_op jit(solution)/shard_map/pallas_call | solution.py:278
  93.6 0.6 copy.9
Async XLA Ops:
  0.0 0.7 copy-start.6
  0.7 1.2 %copy-start = (bf16[1,512,1024]{2,1,0:T(8,128)(2,1)S(1)}, bf16[1,512,1024]{2,1,0:T(8,128)(2,1)}, u32[]{:S(2)}) copy-start(bf16[1,512,1024]{2,1,0:T(8,128)(2,1)} %gate_ref.1) | copy-start | bytes 3145732
  1.9 1.2 %copy-start.1 = (bf16[1,512,1024]{2,1,0:T(8,128)(2,1)S(1)}, bf16[1,512,1024]{2,1,0:T(8,128)(2,1)}, u32[]{:S(2)}) copy-start(bf16[1,512,1024]{2,1,0:T(8,128)(2,1)} %up_ref.1) | copy-start | bytes 3145732
  3.1 1.2 %copy-start.2 = (bf16[1,1024,512]{2,1,0:T(8,128)(2,1)S(1)}, bf16[1,1024,512]{2,1,0:T(8,128)(2,1)}, u32[]{:S(2)}) copy-start(bf16[1,1024,512]{2,1,0:T(8,128)(2,1)} %down_ref.1) | copy-start | bytes 3145732
  4.3 0.8 copy-start.3
  5.1 0.8 copy-start.4
  5.8 0.7 copy-start.5

commit v2 on v1

v2 whole, which is shorter than its diff:
```python
import functools
import math

import jax
import jax.numpy as jnp
from jax import lax
from jax.experimental import pallas as pl
from jax.experimental.pallas import tpu as pltpu
from jax.sharding import PartitionSpec as P

BF16, F32, I32 = jnp.bfloat16, jnp.float32, jnp.int32
MESH = pl.DeviceIdType.MESH


TREE = "two"


def parents(tree, length):
    if tree == "ring":
        return {d: d - 1 for d in range(1, length + 1)}
    if tree == "direct":
        return {d: 0 for d in range(1, length + 1)}
    return {d: 0 if d <= 2 else 2 for d in range(1, length + 1)}


def kernel(n, zhi, cap, tree, ids_hbm, rw_hbm, owner_hbm, tok_hbm, gate_ref, up_ref, down_ref, out_ref,
           ids_ref, rw_ref, owner_ref, tok_ref, w1, w2, stage, tok, sel, sel_t, wcol, hid, psend, precv, zsend, zrecv, acc, rbuf, tot, fsend, frecv,
           i_sem, w_sem, d_sem, f_send, f_recv, s_send, s_recv, c_send, c_recv, q_send, q_recv,
           h_send, h_recv, k_send, k_recv, r_send, r_recv, g_send, g_recv):
    rows, feat = tok_ref.shape
    ff = down_ref.shape[1]
    half = ff // 2
    part = half // zhi
    pair = 2 * rows
    block = n * pair
    chunk = block // 2
    total_rows = n * block
    grp, tp = lax.axis_index("grp"), lax.axis_index("tp")
    x, zlo, y = lax.rem(grp, n), lax.rem(lax.div(grp, n), 2), lax.div(grp, 2 * n)
    zh, core = lax.div(tp, 2), lax.rem(tp, 2)
    f = x * (1 - core) + y * core
    s = y * (1 - core) + x * core

    def at(f_, s_, z_):
        y_ = s_ * (1 - core) + f_ * core
        x_ = f_ * (1 - core) + s_ * core
        return ((y_ * 2 + z_) * n + x_, tp)

    def other_z(dz):
        return zlo + dz - 2 * zlo * dz

    near = [(k, dz) for k in range(n) for dz in range(2)][1:]
    f_peer = {(k, dz): at(lax.rem(f + k, n), s, other_z(dz)) for k, dz in near}
    ways = [(w, direction, c) for c in range(2) for w, direction in enumerate((1, -1))]

    def hops(direction, c):
        return n // 2 if (direction > 0) == (c == 0) else n // 2 - 1

    def from_(direction, c):
        return parents(tree, hops(direction, c))

    steps = sorted({d - p for w, direction, c in ways for d, p in from_(direction, c).items()})
    s_peer = {sign * d: at(f, lax.rem(s + n + sign * d, n), zlo) for d in steps for sign in (1, -1)}
    if 2 * max(steps) == n:
        del s_peer[-max(steps)]

    def s_to(d):
        return s_peer[d] if d in s_peer else s_peer[-d]

    sibling = (grp, zh * 2 + (1 - core))
    q_peer = [None] + [(grp, lax.rem(zh + j, zhi) * 2 + core) for j in range(1, zhi)]

    def send(src, dst, ssem, rsem, device):
        copy = pltpu.make_async_remote_copy(src_ref=src, dst_ref=dst, send_sem=ssem, recv_sem=rsem,
                                            device_id=device, device_id_type=MESH)
        copy.start()
        return copy

    def arrived(dst, ssem, rsem, device):
        pltpu.make_async_remote_copy(src_ref=dst, dst_ref=dst, send_sem=ssem, recv_sem=rsem,
                                     device_id=device, device_id_type=MESH).wait_recv()

    sent = []

    peers = list(f_peer.values()) + list(s_peer.values()) + [sibling] + q_peer[1:]
    barrier = pltpu.get_barrier_semaphore()
    for peer in peers:
        pl.semaphore_signal(barrier, inc=1, device_id=peer, device_id_type=MESH)

    small = []
    for m, (src, dst) in enumerate(((tok_hbm, tok_ref), (ids_hbm, ids_ref), (rw_hbm, rw_ref), (owner_hbm, owner_ref))):
        load = pltpu.make_async_copy(src, dst, i_sem.at[m])
        load.start()
        small.append(load)

    loads = []
    for slot in range(2):
        side = (1 - core) if slot == 0 else core
        for q in range(zhi):
            for m, ref in enumerate((gate_ref, up_ref)):
                column = pl.multiple_of(side * half + q * part, part)
                load = pltpu.make_async_copy(ref.at[0, :, pl.ds(column, part)],
                                             w1.at[slot, q, :, pl.ds(m * part, part)], w_sem.at[slot, q, m])
                load.start()
                loads.append(load)
    load_down = pltpu.make_async_copy(down_ref.at[0], w2, d_sem)
    load_down.start()

    for load in small:
        load.wait()
    pl.semaphore_wait(barrier, len(peers))

    def fold(v):
        return jnp.concatenate([v[..., :feat // 2], v[..., feat // 2:]], axis=-2)

    def unfold(v):
        return jnp.concatenate([v[..., :rows, :], v[..., rows:, :]], axis=-1)

    mine2 = f * 2 + zlo
    stage[mine2] = fold(tok_ref[...].astype(F32)).astype(BF16)
    for m, (k, dz) in enumerate(near):
        sent.append(send(stage.at[mine2], stage.at[mine2], f_send.at[m], f_recv.at[m], f_peer[k, dz]))

    experts = owner_ref.shape[1]
    mine = jnp.sum(jnp.where(owner_ref[...] == grp, lax.broadcasted_iota(I32, (1, experts), 1), 0),
                   axis=1, keepdims=True)
    hit = ids_ref[...] == mine
    taken = jnp.max(jnp.where(hit, 1.0, 0.0), axis=0, keepdims=True)
    weight = jnp.sum(jnp.where(hit, rw_ref[...], 0.0), axis=0, keepdims=True)
    high = weight.astype(BF16).astype(F32)
    middle = (weight - high).astype(BF16).astype(F32)
    low = weight - high - middle
    lanes = block

    def square(v):
        wide = jnp.broadcast_to(v, (n, total_rows))
        at_row = lax.broadcasted_iota(I32, (n, lanes), 0)
        return sum(jnp.where(at_row == a, wide[:, a * lanes:(a + 1) * lanes], 0.0) for a in range(n))

    taken_sq = square(taken)
    before = jnp.where(lax.broadcasted_iota(I32, (lanes, lanes), 0) < lax.broadcasted_iota(I32, (lanes, lanes), 1),
                       1.0, 0.0).astype(BF16)
    in_line = jnp.dot(taken_sq.astype(BF16), before, preferred_element_type=F32)
    counts = jnp.sum(taken_sq, axis=1, keepdims=True)
    ahead = jnp.zeros((n, lanes), F32)
    at_row = lax.broadcasted_iota(I32, (n, lanes), 0)
    for a in range(n - 1):
        ahead += jnp.where(at_row > a, counts[a:a + 1, :], 0.0)
    place_sq = jnp.where(taken_sq > 0.5, in_line + ahead, -1.0)
    stacked = jnp.concatenate([place_sq, square(high), square(middle), square(low)], axis=0).astype(BF16)
    position = lax.broadcasted_iota(I32, (1, total_rows), 1)
    bits = [int(math.log2(v)) for v in (rows, n)]
    i_ = position & (rows - 1)
    z_ = lax.shift_right_logical(position, bits[0]) & 1
    f_ = lax.shift_right_logical(position, bits[0] + 1) & (n - 1)
    s_ = lax.shift_right_logical(position, bits[0] + 1 + bits[1])
    y_ = s_ * (1 - core) + f_ * core
    x_ = f_ * (1 - core) + s_ * core
    lane_of = (z_ * n + x_) * rows + i_
    take = jnp.where(lax.broadcasted_iota(I32, (lanes, total_rows), 0) == lane_of, 1.0, 0.0).astype(BF16)
    spread_out = jnp.dot(stacked, take, preferred_element_type=F32)
    keep = lax.broadcasted_iota(I32, (n, total_rows), 0) == y_

    def line(m):
        return jnp.sum(jnp.where(keep, spread_out[m * n:(m + 1) * n], 0.0), axis=0, keepdims=True)

    place_of = line(0)
    weight_at = line(1) + line(2) + line(3)
    slot_at = lax.broadcasted_iota(I32, (cap, block), 0).astype(F32)
    weights = jnp.zeros((cap, block), F32)
    for t in range(n):
        here = slice(t * block, (t + 1) * block)
        one = jnp.where(place_of[:, here] == slot_at, 1.0, 0.0)
        sel[t] = one.astype(BF16)
        weights += one * weight_at[:, here]
    wcol[...] = jnp.broadcast_to(jnp.sum(weights, axis=1, keepdims=True), wcol.shape)

    for m, (k, dz) in enumerate(near):
        came = lax.rem(f + n - k, n) * 2 + other_z(dz)
        arrived(stage.at[came], f_send.at[m], f_recv.at[m], f_peer[k, dz])
    tok[pl.ds(pl.multiple_of(s * block, block), block), :] = (
        unfold(stage[...].astype(F32)).reshape(block, feat).astype(BF16))

    def at_chunk(s_, c):
        return pl.ds(pl.multiple_of(s_ * block + c * chunk, chunk), chunk)

    order_out = sorted(range(1, n // 2 + 1), key=lambda d: (d not in parents(tree, n // 2).values(), -d))

    def hand_out(d, those):
        for e in order_out:
            for w, direction, c in those:
                if from_(direction, c).get(e) == d:
                    held = at_chunk(lax.rem(s + n - direction * d, n), c)
                    sent.append(send(tok.at[held], tok.at[held], s_send.at[w, c, e - 1], s_recv.at[w, c, e - 1],
                                     s_to(direction * (e - d))))

    hand_out(0, ways)

    def rows_of(*ts):
        return jnp.dot(jnp.concatenate([sel[t] for t in ts], axis=1),
                       jnp.concatenate([tok[pl.ds(pl.multiple_of(t * block, block), block), :] for t in ts], axis=0),
                       preferred_element_type=F32)

    picked = None
    for h in sorted(range(1, n // 2 + 1), key=lambda d: (d not in parents(tree, n // 2).values(), d)):
        for w, direction, c in ways:
            if h <= hops(direction, c):
                came = at_chunk(lax.rem(s + n - direction * h, n), c)
                arrived(tok.at[came], s_send.at[w, c, h - 1], s_recv.at[w, c, h - 1], s_to(direction))
                hand_out(h, [(w, direction, c)])
        more = rows_of(lax.rem(s + h, n), s if h == n // 2 else lax.rem(s + n - h, n))
        picked = more if picked is None else picked + more
    rows_x = picked.astype(BF16)

    for load in loads:
        load.wait()
    order = [1] if zhi == 2 else [2, 1, 3]
    order = order + [0]

    def for_sibling(j):
        psend[j] = jnp.dot(rows_x, w1[0, lax.rem(zh + j, zhi)], preferred_element_type=F32)
        sent.append(send(psend.at[j], precv.at[j], c_send.at[j], c_recv.at[j], sibling))

    own = None
    for_sibling(order[0])
    for m, j in enumerate(order):
        if m + 1 < zhi:
            for_sibling(order[m + 1])
        product = jnp.dot(rows_x, w1[1, lax.rem(zh + j, zhi)], preferred_element_type=F32)
        arrived(precv.at[j], c_send.at[j], c_recv.at[j], sibling)
        both = product + precv[j]
        if j == 0:
            own = both
        else:
            zsend[j] = both.astype(BF16)
            sent.append(send(zsend.at[j], zrecv.at[j], q_send.at[j], q_recv.at[j], q_peer[j]))

    for t in range(n):
        sel_t[t] = sel[t].astype(F32).T.astype(BF16)
    load_down.wait()
    for j in order[:-1][::-1]:
        arrived(zrecv.at[j], q_send.at[j], q_recv.at[j], q_peer[j])
        own += zrecv[j].astype(F32)
    gate, up = own[:, :part], own[:, part:]
    me = core * zhi + zh
    hid[me] = (gate / (1.0 + jnp.exp(-gate)) * up).astype(BF16)

    for j in order[:-1]:
        sent.append(send(hid.at[me], hid.at[me], h_send.at[j], h_recv.at[j], q_peer[j]))
    sent.append(send(hid.at[me], hid.at[me], k_send.at[0], k_recv.at[0], sibling))

    def down(*ms):
        return jnp.dot(jnp.concatenate([hid[m] for m in ms], axis=1),
                       jnp.concatenate([w2[pl.ds(pl.multiple_of(m * part, part), part), :] for m in ms], axis=0),
                       preferred_element_type=F32)

    theirs = (1 - core) * zhi
    for j in order[:-1][::-1]:
        came = core * zhi + lax.rem(zh + zhi - j, zhi)
        arrived(hid.at[came], h_send.at[j], h_recv.at[j], q_peer[j])
        sent.append(send(hid.at[came], hid.at[came], k_send.at[j], k_recv.at[j], sibling))
    result = None
    for j in order[::-1]:
        q = lax.rem(zh + zhi - j, zhi)
        arrived(hid.at[theirs + q], k_send.at[j], k_recv.at[j], sibling)
        more = down(core * zhi + q, theirs + q)
        result = more if result is None else result + more
    result = (result * wcol[:, 0:1]).astype(BF16)

    def spread(t):
        acc[pl.ds(pl.multiple_of(t * block, block), block), :] = jnp.dot(
            sel_t[t], result, preferred_element_type=F32).astype(BF16)

    def take_in(w, direction, c, d, onto):
        for e, p in from_(direction, c).items():
            if p == d:
                arrived(rbuf.at[w, c, e - 1], r_send.at[w, c, e - 1], r_recv.at[w, c, e - 1], s_to(direction))
                onto += rbuf[w, c, e - 1].astype(F32)
        return onto

    def pass_on(w, direction, c, d):
        of = at_chunk(lax.rem(s + n - direction * d, n), c)
        p = from_(direction, c)[d]
        if d in from_(direction, c).values():
            acc[of, :] = take_in(w, direction, c, d, acc[of, :].astype(F32)).astype(BF16)
        sent.append(send(acc.at[of], rbuf.at[w, c, d - 1], r_send.at[w, c, d - 1], r_recv.at[w, c, d - 1],
                         s_to(-direction * (d - p))))

    for d in range(n // 2, 0, -1):
        spread(lax.rem(s + d, n))
        if d < n // 2:
            spread(lax.rem(s + n - d, n))
        for w, direction, c in ways:
            if d <= hops(direction, c) and d not in from_(direction, c).values():
                pass_on(w, direction, c, d)
    spread(s)
    for d in range(n // 2, 0, -1):
        for w, direction, c in ways:
            if d <= hops(direction, c) and d in from_(direction, c).values():
                pass_on(w, direction, c, d)
    for c in range(2):
        summed = acc[at_chunk(s, c), :].astype(F32)
        for w, direction in enumerate((1, -1)):
            summed = take_in(w, direction, c, 0, summed)
        tot[c * chunk:(c + 1) * chunk, :] = summed

    fsend[...] = fold(tot[...].reshape(2 * n, rows, feat)).astype(BF16)
    for m, (k, dz) in enumerate(near):
        to = lax.rem(f + k, n) * 2 + other_z(dz)
        sent.append(send(fsend.at[to], frecv.at[m], g_send.at[m], g_recv.at[m], f_peer[k, dz]))
    summed = jnp.zeros((2 * rows, feat // 2), F32)
    for m, (k, dz) in enumerate(near):
        arrived(frecv.at[m], g_send.at[m], g_recv.at[m], f_peer[k, dz])
        summed += frecv[m].astype(F32)
    own8 = tot[pl.ds(pl.multiple_of(mine2 * rows, rows), rows), :]
    out_ref[...] = (own8 + unfold(summed)).astype(out_ref.dtype)

    for copy in sent:
        copy.wait_send()


def on_device(n, zhi, tokens, expert_ids, route_weight, owner, gate_weight, up_weight, down_weight):
    rows, feat = tokens.shape
    total_rows = expert_ids.shape[0]
    ff = gate_weight.shape[2]
    part = ff // 2 // zhi
    cap = min(20 * rows, total_rows)
    pair = 2 * rows
    block = n * pair
    chunk = block // 2
    half_ring = max(n // 2, 1)
    dma = pltpu.SemaphoreType.DMA
    vmem = pl.BlockSpec(memory_space=pltpu.VMEM)
    hbm = pl.BlockSpec(memory_space=pl.ANY)
    return pl.pallas_call(
        functools.partial(kernel, n, zhi, cap, TREE),
        out_shape=jax.ShapeDtypeStruct((rows, feat), BF16),
        in_specs=[hbm] * 7,
        out_specs=vmem,
        scratch_shapes=[
            pltpu.VMEM(expert_ids.shape[::-1], I32),
            pltpu.VMEM(route_weight.shape[::-1], F32),
            pltpu.VMEM((1, owner.shape[0]), I32),
            pltpu.VMEM((rows, feat), BF16),
            pltpu.VMEM((2, zhi, feat, 2 * part), BF16),
            pltpu.VMEM((ff, feat), BF16),
            pltpu.VMEM((2 * n, pair, feat // 2), BF16),
            pltpu.VMEM((total_rows, feat), BF16),
            pltpu.VMEM((n, cap, block), BF16),
            pltpu.VMEM((n, block, cap), BF16),
            pltpu.VMEM((cap, 128), F32),
            pltpu.VMEM((2 * zhi, cap, part), BF16),
            pltpu.VMEM((zhi, cap, 2 * part), F32),
            pltpu.VMEM((zhi, cap, 2 * part), F32),
            pltpu.VMEM((zhi, cap, 2 * part), BF16),
            pltpu.VMEM((zhi, cap, 2 * part), BF16),
            pltpu.VMEM((total_rows, feat), BF16),
            pltpu.VMEM((2, 2, half_ring, chunk, feat), BF16),
            pltpu.VMEM((block, feat), F32),
            pltpu.VMEM((2 * n, pair, feat // 2), BF16),
            pltpu.VMEM((2 * n - 1, pair, feat // 2), BF16),
            dma((4,)), dma((2, zhi, 2)), dma,
            dma((2 * n - 1,)), dma((2 * n - 1,)),
            dma((2, 2, half_ring)), dma((2, 2, half_ring)),
            dma((zhi,)), dma((zhi,)),
            dma((zhi,)), dma((zhi,)),
            dma((zhi,)), dma((zhi,)),
            dma((zhi,)), dma((zhi,)),
            dma((2, 2, half_ring)), dma((2, 2, half_ring)),
            dma((2 * n - 1,)), dma((2 * n - 1,)),
        ],
        compiler_params=pltpu.CompilerParams(
            collective_id=0, has_side_effects=True, vmem_limit_bytes=60 * 1024 * 1024
        ),
        cost_estimate=pl.CostEstimate(flops=2 * cap * feat * ff * 3, bytes_accessed=6 * feat * ff,
                                      transcendentals=cap * ff // 8),
    )(expert_ids.T, route_weight.T, owner.reshape(1, -1), tokens, gate_weight, up_weight, down_weight)


def solution(mesh):
    n = math.isqrt(mesh.shape["grp"] // 2)
    return jax.shard_map(
        functools.partial(on_device, n, mesh.shape["tp"] // 2),
        mesh=mesh,
        in_specs=(
            P("grp", "tp"),
            P(),
            P(),
            P(),
            P("grp", "tp", None),
            P("grp", "tp", None),
            P("grp", None, "tp"),
        ),
        out_specs=P("grp", "tp"),
        check_vma=False,
    )
```

time: 94.7 us -> 77.8 us (0.82)
  the two profiles are of different devices: /device:TPU:128 before, /device:TPU:1 now
where the time goes in v2:
time: 77.8 us; the launch traced here: 76.7 us
  Pallas kernels  75.4 us (97%)
  local copies, waits for them, and re-layouts  1.3 us (2%)
    pallas_call x1, Pallas kernels, on_device(): pl.pallas_call(functools.partial(kernel, n, zhi, cap, TREE), out_shape=ja...  75.4 us

profile of v2, /device:TPU:1, one launch (start us, length us, event | category | flops | bytes accessed | tf_op | source)
XLA Modules:
  0.0 76.7 jit_solution(10966959612938080702)
XLA Ops:
  0.0 75.4 %shard_map.73 = bf16[8,512]{1,0:T(8,128)(2,1)} custom-call(s32[8,1024]{1,0:T(8,128)} %bitcast.3, f32[8,1024]{1,0:T(8,128)} %bitcast.4, s32[1,128]{1,0:T(1,128)} %bitcast.5, bf16[8,512]{1,0:T(8,128)(2,1)} %tok_hbm.1, bf16[1,512,1024]{2,1,0:T(8,128)(2,1)} %gate_ref.1, bf16[1,512,1024]{2,1,0:T(8,128)(2,1)} %up_ref.1, bf16[1,1024,512]{2,1,0:T(8,128)(2,1)} %down_ref.1), custom_call_target="tpu_custom_call" | custom-call | flops 503316480 | bytes 3145728 | tf_op jit(solution)/shard_map/pallas_call | solution.py:335
  75.4 1.3 %copy.9 = bf16[8,512]{1,0:T(8,128)(2,1)} copy(bf16[8,512]{1,0:T(8,128)(2,1)} %shard_map.73) | data formatting | bytes 16384

commit v3 on v2

--- a/solution.py
+++ b/solution.py
@@ -13,6 +13,7 @@
 
 
 TREE = "two"
+CHUNKS = 4
 
 
 def parents(tree, length):
@@ -33,28 +34,29 @@
     part = half // zhi
     pair = 2 * rows
     block = n * pair
-    chunk = block // 2
+    chunk = block // CHUNKS
     total_rows = n * block
     grp, tp = lax.axis_index("grp"), lax.axis_index("tp")
     x, zlo, y = lax.rem(grp, n), lax.rem(lax.div(grp, n), 2), lax.div(grp, 2 * n)
     zh, core = lax.div(tp, 2), lax.rem(tp, 2)
-    f = x * (1 - core) + y * core
-    s = y * (1 - core) + x * core
+    turn = core
+    f = x * (1 - turn) + y * turn
+    s = y * (1 - turn) + x * turn
 
     def at(f_, s_, z_):
-        y_ = s_ * (1 - core) + f_ * core
-        x_ = f_ * (1 - core) + s_ * core
+        y_ = s_ * (1 - turn) + f_ * turn
+        x_ = f_ * (1 - turn) + s_ * turn
         return ((y_ * 2 + z_) * n + x_, tp)
 
     def other_z(dz):
         return zlo + dz - 2 * zlo * dz
 
-    near = [(k, dz) for k in range(n) for dz in range(2)][1:]
+    near = sorted([(k, dz) for k in range(n) for dz in range(2)][1:], key=lambda v: -min(v[0], n - v[0]) - v[1])
     f_peer = {(k, dz): at(lax.rem(f + k, n), s, other_z(dz)) for k, dz in near}
-    ways = [(w, direction, c) for c in range(2) for w, direction in enumerate((1, -1))]
+    ways = [(w, direction, c) for c in range(CHUNKS) for w, direction in enumerate((1, -1))]
 
     def hops(direction, c):
-        return n // 2 if (direction > 0) == (c == 0) else n // 2 - 1
+        return n // 2 if (direction > 0) == (c % 2 == 0) else n // 2 - 1
 
     def from_(direction, c):
         return parents(tree, hops(direction, c))
@@ -82,34 +84,17 @@
 
     sent = []
 
-    peers = list(f_peer.values()) + list(s_peer.values()) + [sibling] + q_peer[1:]
+    def load(src, dst, sem):
+        copy = pltpu.make_async_copy(src, dst, sem)
+        copy.start()
+        return copy
+
+    rows_in = load(tok_hbm, tok_ref, i_sem.at[0])
+    peers = list(f_peer.values()) + list(s_peer.values()) + q_peer[1:] + [sibling]
     barrier = pltpu.get_barrier_semaphore()
     for peer in peers:
         pl.semaphore_signal(barrier, inc=1, device_id=peer, device_id_type=MESH)
 
-    small = []
-    for m, (src, dst) in enumerate(((tok_hbm, tok_ref), (ids_hbm, ids_ref), (rw_hbm, rw_ref), (owner_hbm, owner_ref))):
-        load = pltpu.make_async_copy(src, dst, i_sem.at[m])
-        load.start()
-        small.append(load)
-
-    loads = []
-    for slot in range(2):
-        side = (1 - core) if slot == 0 else core
-        for q in range(zhi):
-            for m, ref in enumerate((gate_ref, up_ref)):
-                column = pl.multiple_of(side * half + q * part, part)
-                load = pltpu.make_async_copy(ref.at[0, :, pl.ds(column, part)],
-                                             w1.at[slot, q, :, pl.ds(m * part, part)], w_sem.at[slot, q, m])
-                load.start()
-                loads.append(load)
-    load_down = pltpu.make_async_copy(down_ref.at[0], w2, d_sem)
-    load_down.start()
-
-    for load in small:
-        load.wait()
-    pl.semaphore_wait(barrier, len(peers))
-
     def fold(v):
         return jnp.concatenate([v[..., :feat // 2], v[..., feat // 2:]], axis=-2)
 
@@ -117,9 +102,18 @@
         return jnp.concatenate([v[..., :rows, :], v[..., rows:, :]], axis=-1)
 
     mine2 = f * 2 + zlo
+    rows_in.wait()
     stage[mine2] = fold(tok_ref[...].astype(F32)).astype(BF16)
+    pl.semaphore_wait(barrier, len(peers))
     for m, (k, dz) in enumerate(near):
         sent.append(send(stage.at[mine2], stage.at[mine2], f_send.at[m], f_recv.at[m], f_peer[k, dz]))
+
+    small = [load(ids_hbm, ids_ref, i_sem.at[1]), load(rw_hbm, rw_ref, i_sem.at[2]),
+             load(owner_hbm, owner_ref, i_sem.at[3])]
+    loads = [load(gate_ref.at[0], w1.at[0], w_sem.at[0]), load(up_ref.at[0], w1.at[1], w_sem.at[1])]
+    load_down = load(down_ref.at[0], w2, d_sem)
+    for copy in small:
+        copy.wait()
 
     experts = owner_ref.shape[1]
     mine = jnp.sum(jnp.where(owner_ref[...] == grp, lax.broadcasted_iota(I32, (1, experts), 1), 0),
@@ -154,8 +148,8 @@
     z_ = lax.shift_right_logical(position, bits[0]) & 1
     f_ = lax.shift_right_logical(position, bits[0] + 1) & (n - 1)
     s_ = lax.shift_right_logical(position, bits[0] + 1 + bits[1])
-    y_ = s_ * (1 - core) + f_ * core
-    x_ = f_ * (1 - core) + s_ * core
+    y_ = s_ * (1 - turn) + f_ * turn
+    x_ = f_ * (1 - turn) + s_ * turn
     lane_of = (z_ * n + x_) * rows + i_
     take = jnp.where(lax.broadcasted_iota(I32, (lanes, total_rows), 0) == lane_of, 1.0, 0.0).astype(BF16)
     spread_out = jnp.dot(stacked, take, preferred_element_type=F32)
@@ -212,13 +206,18 @@
         picked = more if picked is None else picked + more
     rows_x = picked.astype(BF16)
 
-    for load in loads:
-        load.wait()
+    for copy in loads:
+        copy.wait()
     order = [1] if zhi == 2 else [2, 1, 3]
     order = order + [0]
 
+    def partial(side, j):
+        columns = pl.ds(pl.multiple_of(side * half + lax.rem(zh + j, zhi) * part, part), part)
+        return jnp.dot(rows_x, jnp.concatenate([w1[0, :, columns], w1[1, :, columns]], axis=1),
+                       preferred_element_type=F32)
+
     def for_sibling(j):
-        psend[j] = jnp.dot(rows_x, w1[0, lax.rem(zh + j, zhi)], preferred_element_type=F32)
+        psend[j] = partial(1 - core, j)
         sent.append(send(psend.at[j], precv.at[j], c_send.at[j], c_recv.at[j], sibling))
 
     own = None
@@ -226,7 +225,7 @@
     for m, j in enumerate(order):
         if m + 1 < zhi:
             for_sibling(order[m + 1])
-        product = jnp.dot(rows_x, w1[1, lax.rem(zh + j, zhi)], preferred_element_type=F32)
+        product = partial(core, j)
         arrived(precv.at[j], c_send.at[j], c_recv.at[j], sibling)
         both = product + precv[j]
         if j == 0:
@@ -298,7 +297,7 @@
         for w, direction, c in ways:
             if d <= hops(direction, c) and d in from_(direction, c).values():
                 pass_on(w, direction, c, d)
-    for c in range(2):
+    for c in range(CHUNKS):
         summed = acc[at_chunk(s, c), :].astype(F32)
         for w, direction in enumerate((1, -1)):
             summed = take_in(w, direction, c, 0, summed)
@@ -327,7 +326,7 @@
     cap = min(20 * rows, total_rows)
     pair = 2 * rows
     block = n * pair
-    chunk = block // 2
+    chunk = block // CHUNKS
     half_ring = max(n // 2, 1)
     dma = pltpu.SemaphoreType.DMA
     vmem = pl.BlockSpec(memory_space=pltpu.VMEM)
@@ -342,7 +341,7 @@
             pltpu.VMEM(route_weight.shape[::-1], F32),
             pltpu.VMEM((1, owner.shape[0]), I32),
             pltpu.VMEM((rows, feat), BF16),
-            pltpu.VMEM((2, zhi, feat, 2 * part), BF16),
+            pltpu.VMEM((2, feat, ff), BF16),
             pltpu.VMEM((ff, feat), BF16),
             pltpu.VMEM((2 * n, pair, feat // 2), BF16),
             pltpu.VMEM((total_rows, feat), BF16),
@@ -355,22 +354,22 @@
             pltpu.VMEM((zhi, cap, 2 * part), BF16),
             pltpu.VMEM((zhi, cap, 2 * part), BF16),
             pltpu.VMEM((total_rows, feat), BF16),
-            pltpu.VMEM((2, 2, half_ring, chunk, feat), BF16),
+            pltpu.VMEM((2, CHUNKS, half_ring, chunk, feat), BF16),
             pltpu.VMEM((block, feat), F32),
             pltpu.VMEM((2 * n, pair, feat // 2), BF16),
             pltpu.VMEM((2 * n - 1, pair, feat // 2), BF16),
-            dma((4,)), dma((2, zhi, 2)), dma,
+            dma((4,)), dma((2,)), dma,
             dma((2 * n - 1,)), dma((2 * n - 1,)),
-            dma((2, 2, half_ring)), dma((2, 2, half_ring)),
+            dma((2, CHUNKS, half_ring)), dma((2, CHUNKS, half_ring)),
             dma((zhi,)), dma((zhi,)),
             dma((zhi,)), dma((zhi,)),
             dma((zhi,)), dma((zhi,)),
             dma((zhi,)), dma((zhi,)),
-            dma((2, 2, half_ring)), dma((2, 2, half_ring)),
+            dma((2, CHUNKS, half_ring)), dma((2, CHUNKS, half_ring)),
             dma((2 * n - 1,)), dma((2 * n - 1,)),
         ],
         compiler_params=pltpu.CompilerParams(
-            collective_id=0, has_side_effects=True, vmem_limit_bytes=60 * 1024 * 1024
+            collective_id=0, has_side_effects=True, vmem_limit_bytes=55216 * 1024
         ),
         cost_estimate=pl.CostEstimate(flops=2 * cap * feat * ff * 3, bytes_accessed=6 * feat * ff,
                                       transcendentals=cap * ff // 8),

time: 77.8 us -> 76.6 us (0.985); the launches traced: 76.7 us -> 76.4 us
  no operation moved by 1% of the time
where the time goes in v3:
time: 76.6 us; the launch traced here: 76.4 us
  Pallas kernels  75.2 us (98%)
  local copies, waits for them, and re-layouts  1.26 us (2%)
    pallas_call x1, Pallas kernels, on_device(): pl.pallas_call(functools.partial(kernel, n, zhi, cap, TREE), out_shape=ja...  75.2 us

profile of v3, /device:TPU:1, one launch (start us, length us, event | category | flops | bytes accessed | tf_op | source)
XLA Modules:
  0.0 76.4 jit_solution(13889694953726936959)
XLA Ops:
  0.0 0.0 copy-start
  0.0 0.7 copy-done
  0.7 75.2 %shard_map.73 = bf16[8,512]{1,0:T(8,128)(2,1)S(1)} custom-call(s32[8,1024]{1,0:T(8,128)} %bitcast.4, f32[8,1024]{1,0:T(8,128)} %bitcast.5, s32[1,128]{1,0:T(1,128)S(1)} %bitcast.3, bf16[8,512]{1,0:T(8,128)(2,1)} %tok_hbm.1, bf16[1,512,1024]{2,1,0:T(8,128)(2,1)} %gate_ref.1, bf16[1,512,1024]{2,1,0:T(8,128)(2,1)} %up_ref.1, bf16[1,1024,512]{2,1,0:T(8,128)(2,1)} %down_ref.1), custom_call_target="tpu_custom_call" | custom-call | flops 503316480 | bytes 3145728 | tf_op jit(solution)/shard_map/pallas_call | solution.py:334
  75.8 0.6 copy.9
Async XLA Ops:
  0.0 0.7 copy-start

commit v4 on v3

--- a/solution.py
+++ b/solution.py
@@ -175,6 +175,15 @@
     tok[pl.ds(pl.multiple_of(s * block, block), block), :] = (
         unfold(stage[...].astype(F32)).reshape(block, feat).astype(BF16))
 
+    def whole(direction, c, e):
+        tree_ = from_(direction, c)
+        return tree_.get(e) == 0 and e not in tree_.values() and 2 * e < n - 2
+
+    def piece(s_, direction, c, e):
+        if whole(direction, c, e):
+            return pl.ds(pl.multiple_of(s_ * block, block), block)
+        return at_chunk(s_, c)
+
     def at_chunk(s_, c):
         return pl.ds(pl.multiple_of(s_ * block + c * chunk, chunk), chunk)
 
@@ -183,8 +192,8 @@
     def hand_out(d, those):
         for e in order_out:
             for w, direction, c in those:
-                if from_(direction, c).get(e) == d:
-                    held = at_chunk(lax.rem(s + n - direction * d, n), c)
+                if from_(direction, c).get(e) == d and not (c and whole(direction, c, e)):
+                    held = piece(lax.rem(s + n - direction * d, n), direction, c, e)
                     sent.append(send(tok.at[held], tok.at[held], s_send.at[w, c, e - 1], s_recv.at[w, c, e - 1],
                                      s_to(direction * (e - d))))
 
@@ -198,8 +207,8 @@
     picked = None
     for h in sorted(range(1, n // 2 + 1), key=lambda d: (d not in parents(tree, n // 2).values(), d)):
         for w, direction, c in ways:
-            if h <= hops(direction, c):
-                came = at_chunk(lax.rem(s + n - direction * h, n), c)
+            if h <= hops(direction, c) and not (c and whole(direction, c, h)):
+                came = piece(lax.rem(s + n - direction * h, n), direction, c, h)
                 arrived(tok.at[came], s_send.at[w, c, h - 1], s_recv.at[w, c, h - 1], s_to(direction))
                 hand_out(h, [(w, direction, c)])
         more = rows_of(lax.rem(s + h, n), s if h == n // 2 else lax.rem(s + n - h, n))
@@ -270,20 +279,27 @@
         acc[pl.ds(pl.multiple_of(t * block, block), block), :] = jnp.dot(
             sel_t[t], result, preferred_element_type=F32).astype(BF16)
 
+    def landing(direction, c, e):
+        return pl.ds(0, block) if whole(direction, c, e) else pl.ds(c * chunk, chunk)
+
     def take_in(w, direction, c, d, onto):
         for e, p in from_(direction, c).items():
             if p == d:
-                arrived(rbuf.at[w, c, e - 1], r_send.at[w, c, e - 1], r_recv.at[w, c, e - 1], s_to(direction))
-                onto += rbuf[w, c, e - 1].astype(F32)
+                if not (c and whole(direction, c, e)):
+                    arrived(rbuf.at[w, e - 1, landing(direction, c, e)], r_send.at[w, c, e - 1],
+                            r_recv.at[w, c, e - 1], s_to(direction))
+                onto += rbuf[w, e - 1, c * chunk:(c + 1) * chunk].astype(F32)
         return onto
 
     def pass_on(w, direction, c, d):
-        of = at_chunk(lax.rem(s + n - direction * d, n), c)
+        if c and whole(direction, c, d):
+            return
+        of = piece(lax.rem(s + n - direction * d, n), direction, c, d)
         p = from_(direction, c)[d]
         if d in from_(direction, c).values():
             acc[of, :] = take_in(w, direction, c, d, acc[of, :].astype(F32)).astype(BF16)
-        sent.append(send(acc.at[of], rbuf.at[w, c, d - 1], r_send.at[w, c, d - 1], r_recv.at[w, c, d - 1],
-                         s_to(-direction * (d - p))))
+        sent.append(send(acc.at[of], rbuf.at[w, d - 1, landing(direction, c, d)], r_send.at[w, c, d - 1],
+                         r_recv.at[w, c, d - 1], s_to(-direction * (d - p))))
 
     for d in range(n // 2, 0, -1):
         spread(lax.rem(s + d, n))
@@ -354,7 +370,7 @@
             pltpu.VMEM((zhi, cap, 2 * part), BF16),
             pltpu.VMEM((zhi, cap, 2 * part), BF16),
             pltpu.VMEM((total_rows, feat), BF16),
-            pltpu.VMEM((2, CHUNKS, half_ring, chunk, feat), BF16),
+            pltpu.VMEM((2, half_ring, block, feat), BF16),
             pltpu.VMEM((block, feat), F32),
             pltpu.VMEM((2 * n, pair, feat // 2), BF16),
             pltpu.VMEM((2 * n - 1, pair, feat // 2), BF16),

time: 76.6 us -> 76.6 us (level)
  no operation moved by 1% of the time
where the time goes in v4:
time: 76.6 us; the launch traced here: 76.4 us
  Pallas kernels  75.2 us (98%)
  local copies, waits for them, and re-layouts  1.26 us (2%)
    pallas_call x1, Pallas kernels, on_device(): pl.pallas_call(functools.partial(kernel, n, zhi, cap, TREE), out_shape=ja...  75.2 us

profile of v4, /device:TPU:1, one launch (start us, length us, event | category | flops | bytes accessed | tf_op | source)
XLA Modules:
  0.0 76.4 jit_solution(12156151769486812763)
XLA Ops:
  0.0 0.0 copy-start
  0.0 0.7 copy-done
  0.7 75.2 %shard_map.73 = bf16[8,512]{1,0:T(8,128)(2,1)S(1)} custom-call(s32[8,1024]{1,0:T(8,128)} %bitcast.4, f32[8,1024]{1,0:T(8,128)} %bitcast.5, s32[1,128]{1,0:T(1,128)S(1)} %bitcast.3, bf16[8,512]{1,0:T(8,128)(2,1)} %tok_hbm.1, bf16[1,512,1024]{2,1,0:T(8,128)(2,1)} %gate_ref.1, bf16[1,512,1024]{2,1,0:T(8,128)(2,1)} %up_ref.1, bf16[1,1024,512]{2,1,0:T(8,128)(2,1)} %down_ref.1), custom_call_target="tpu_custom_call" | custom-call | flops 503316480 | bytes 3145728 | tf_op jit(solution)/shard_map/pallas_call | solution.py:350
  75.8 0.6 copy.9
Async XLA Ops:
  0.0 0.7 copy-start
